TPU v7x, 256 devices: a whole 4x4x8 slice. The times are simulated.
256 devices in a mesh: blk: 64 (over y, z_hi, x), head: 4 (over z_lo, core).
Axes of the slice: x: 4, y: 4, z: 8 (z_hi: 4, z_lo: 2; z = z_hi * 2 + z_lo), core: 2. Of those that a mesh axis runs over, the one named last changes fastest.
Arguments:
- queries: bfloat16 [49152, 5120], P(('blk', 'head')), may hold values from -6 to 6
- key_input: bfloat16 [49152, 5120], P(('blk', 'head')), may hold values from -6 to 6
- value_input: bfloat16 [49152, 5120], P(('blk', 'head')), may hold values from -6 to 6
- token_order: int32 [49152], P('blk'), may hold values from 0 to 49151, as said below
- tile_mask: int32 [128, 128], P('blk'), may hold values from 0 to 1, as said below
Outputs:
- attended: bfloat16 [49152, 5120], P(('blk', 'head'))
Inputs may be any that keep to these rules, and one draw needn't show every extreme that they name: Within each aligned block of 768 positions, token_order is a permutation of the raster positions of that same block. tile_mask[i, j] is 1 whenever i // 2 = j // 2, and also whenever i // 2 is odd and j = i - 1 or j = i + 1; it is 0 whenever i // 2 and j // 2 differ by more than 1.
All inputs are finite; a program needn't handle non-finite values.
Results may differ from a plain program's by a relative error of at most 0.0047.
Values may be sent and summed in bfloat16 or wider, within the bound.
A program may use at most 128 MiB of HBM per device.

v0:
```python
import math

import jax
import jax.numpy as jnp
from jax import lax
from jax.sharding import PartitionSpec as P

HEAD_DIM = 128


def from_behind(shard, axis, by):
    count = lax.axis_size(axis)
    pairs = [(i, i + by) for i in range(count) if 0 <= i + by < count]
    return lax.ppermute(shard, axis, pairs)


def split_heads(rows, local_heads):
    return jnp.transpose(rows.reshape(rows.shape[0], local_heads, HEAD_DIM), (1, 0, 2))


def local(queries, key_input, value_input, token_order, tile_mask):
    query_rows, key_rows, value_rows = (
        lax.all_to_all(queries, "head", split_axis=1, concat_axis=0, tiled=True),
        lax.all_to_all(key_input, "head", split_axis=1, concat_axis=0, tiled=True),
        lax.all_to_all(value_input, "head", split_axis=1, concat_axis=0, tiled=True),
    )
    group_rows = query_rows.shape[0]
    width = query_rows.shape[1]
    local_heads = width // HEAD_DIM
    tiles_here = tile_mask.shape[0]
    tile_length = group_rows // tiles_here
    scale = 1.0 / math.sqrt(HEAD_DIM)
    block_index = lax.axis_index("blk")
    local_order = token_order - block_index * group_rows
    query_sorted = jnp.take(query_rows, local_order, axis=0)
    key_sorted = jnp.take(key_rows, local_order, axis=0)
    value_sorted = jnp.take(value_rows, local_order, axis=0)
    paired = jnp.stack((key_sorted, value_sorted))
    neighbours = []
    for offset in (1, -1):
        neighbours.append(from_behind(paired, "blk", offset))
    widened = jnp.concatenate((neighbours[0], paired, neighbours[1]), axis=1)
    mask_padded = jnp.pad(tile_mask, ((0, 0), (tiles_here, tiles_here)))
    seen = (
        lax.dynamic_slice(mask_padded, (0, block_index * tiles_here), (tiles_here, 3 * tiles_here))
        > 0
    )
    visible = jnp.repeat(jnp.repeat(seen, tile_length, axis=0), tile_length, axis=1)
    query_heads = split_heads(query_sorted, local_heads)
    key_heads = split_heads(widened[0], local_heads)
    value_heads = split_heads(widened[1], local_heads)

    def one_head(operands):
        query_head, key_head, value_head = operands
        scores = (
            jnp.einsum("qd,kd->qk", query_head, key_head, preferred_element_type=jnp.float32)
            * scale
        )
        scores = jnp.where(visible, scores, -jnp.inf)
        top = jnp.max(scores, axis=1, keepdims=True)
        weights = jnp.exp(scores - top)
        total = jnp.sum(weights, axis=1)
        rounded = weights.astype(jnp.bfloat16)
        mixed = jnp.dot(rounded, value_head, preferred_element_type=jnp.float32)
        return (mixed / total[:, None]).astype(jnp.bfloat16)

    outputs = lax.map(one_head, (query_heads, key_heads, value_heads))
    sorted_out = jnp.transpose(outputs, (1, 0, 2)).reshape(group_rows, width)
    raster = jnp.zeros_like(sorted_out).at[local_order].set(sorted_out)
    return lax.all_to_all(raster, "head", split_axis=0, concat_axis=1, tiled=True)


def solution(mesh):
    in_specs = (
        P(("blk", "head"), None),
        P(("blk", "head"), None),
        P(("blk", "head"), None),
        P("blk"),
        P("blk", None),
    )
    out_specs = P(("blk", "head"), None)
    return jax.shard_map(local, mesh=mesh, in_specs=in_specs, out_specs=out_specs, check_vma=False)
```

profile of v0, /device:TPU:78, one launch (start us, length us, event | category | flops | bytes accessed | tf_op | source)
XLA Modules:
  0.0 439.2 jit_solution(4254503122985430211)
XLA Ops:
  0.0 3.0 copy.51
  3.0 3.6 all-to-all-start
  6.6 2.9 copy.50
  9.5 21.3 %all-to-all-done = bf16[192,4,1280]{2,0,1:T(8,128)(2,1)S(1)} async-done(((bf16[192,4,1280]{2,0,1:T(8,128)(2,1)}), bf16[192,4,1280]{2,0,1:T(8,128)(2,1)S(1)}, u32[]{:S(2)}, u32[]{:S(2)}) %all-to-all-start) | async-done | bytes 1966112 | tf_op jit(solution)/shard_map/all_to_all | solution.py:23
  30.8 4.4 %all-to-all-start.1 = ((bf16[192,4,1280]{2,0,1:T(8,128)(2,1)}), bf16[192,4,1280]{2,0,1:T(8,128)(2,1)}, u32[]{:S(2)}, u32[]{:S(2)}) async-start(bf16[192,4,1280]{2,0,1:T(8,128)(2,1)} %bitcast.76), calls=%async_computation.1 | async-start | bytes 3932160 | tf_op jit(solution)/shard_map/all_to_all | solution.py:24
  35.3 3.0 copy.49
  38.2 21.4 %all-to-all-done.1 = bf16[192,4,1280]{2,0,1:T(8,128)(2,1)} async-done(((bf16[192,4,1280]{2,0,1:T(8,128)(2,1)}), bf16[192,4,1280]{2,0,1:T(8,128)(2,1)}, u32[]{:S(2)}, u32[]{:S(2)}) %all-to-all-start.1) | async-done | bytes 1966112 | tf_op jit(solution)/shard_map/all_to_all | solution.py:24
  59.6 4.6 %all-to-all-start.2 = ((bf16[192,4,1280]{2,0,1:T(8,128)(2,1)}), bf16[192,4,1280]{2,0,1:T(8,128)(2,1)}, u32[]{:S(2)}, u32[]{:S(2)}) async-start(bf16[192,4,1280]{2,0,1:T(8,128)(2,1)} %bitcast.75), calls=%async_computation.2 | async-start | bytes 3932160 | tf_op jit(solution)/shard_map/all_to_all | solution.py:25
  64.2 3.7 gather_fusion
  67.9 7.0 %gather_fusion.1 = bf16[768,1280]{1,0:T(8,128)(2,1)} fusion(bf16[768,1280]{1,0:T(8,128)(2,1)} %bitcast.5, s32[1024]{0:T(1024)S(1)} %pad_clamp_fusion), kind=kCustom, calls=%fused_computation.1.clone | custom fusion | bytes 3935232 | tf_op jit(solution)/shard_map/jit(_take)/gather | solution.py:36
  74.9 13.6 %all-to-all-done.2 = bf16[192,4,1280]{2,0,1:T(8,128)(2,1)} async-done(((bf16[192,4,1280]{2,0,1:T(8,128)(2,1)}), bf16[192,4,1280]{2,0,1:T(8,128)(2,1)}, u32[]{:S(2)}, u32[]{:S(2)}) %all-to-all-start.2) | async-done | bytes 1966112 | tf_op jit(solution)/shard_map/all_to_all | solution.py:25
  88.5 7.0 %gather_fusion.2 = bf16[768,1280]{1,0:T(8,128)(2,1)} fusion(bf16[768,1280]{1,0:T(8,128)(2,1)} %bitcast.8, s32[1024]{0:T(1024)S(1)} %pad_clamp_fusion), kind=kCustom, calls=%fused_computation.2.clone | custom fusion | bytes 3935232 | tf_op jit(solution)/shard_map/jit(_take)/gather | solution.py:37
  95.5 4.6 %select_bitcast_fusion.1 = (bf16[1,768,1280]{2,1,0:T(8,128)(2,1)S(1)}, bf16[1,768,1280]{2,1,0:T(8,128)(2,1)S(1)}, bf16[768,1280]{1,0:T(8,128)(2,1)}) fusion(bf16[768,1280]{1,0:T(8,128)(2,1)} %gather_fusion.1, pred[768]{0:T(1024)(128)(4,1)S(1)} %get-tuple-element.78, bf16[768,1280]{1,0:T(8,128)(2,1)} %gather_fusion.2, bf16[768,1280]{1,0:T(8,128)(2,1)} %gather_fusion), kind=kLoop, calls=%fused_computation.29 | loop fusion | flops 2949120 | bytes 11797248 | tf_op jit(solution)/shard_map/stack | solution.py:38
  100.1 2.5 pad_maximum_fusion.1
  102.7 6.3 %collective-permute-start = (bf16[2,768,1280]{2,1,0:T(8,128)(2,1)}, bf16[2,768,1280]{2,1,0:T(8,128)(2,1)}, u32[]{:S(2)}, u32[]{:S(2)}) collective-permute-start(bf16[2,768,1280]{2,1,0:T(8,128)(2,1)} %pad_maximum_fusion.1), channel_id=1, source_target_pairs={{0,4},{4,8},{8,12},{12,16},{16,20},{20,24},{24,28},{28,32},{32,36}... | collective-permute-start | bytes 11796488 | tf_op jit(solution)/shard_map/ppermute | solution.py:14
  109.0 2.1 collective-permute-start.1
  111.2 4.0 copy.26
  115.2 162.5 %collective-permute-done = bf16[2,768,1280]{2,1,0:T(8,128)(2,1)} collective-permute-done((bf16[2,768,1280]{2,1,0:T(8,128)(2,1)}, bf16[2,768,1280]{2,1,0:T(8,128)(2,1)}, u32[]{:S(2)}, u32[]{:S(2)}) %collective-permute-start) | collective-permute-done | bytes 3932192 | tf_op jit(solution)/shard_map/ppermute | solution.py:14
  277.6 8.1 %collective-permute-done.1 = bf16[2,768,1280]{2,1,0:T(8,128)(2,1)} collective-permute-done((bf16[2,768,1280]{2,1,0:T(8,128)(2,1)}, bf16[2,768,1280]{2,1,0:T(8,128)(2,1)}, u32[]{:S(2)}, u32[]{:S(2)}) %collective-permute-start.1) | collective-permute-done | bytes 3932192 | tf_op jit(solution)/shard_map/ppermute | solution.py:14
  285.8 5.3 %pad_maximum_fusion = bf16[2,2304,1280]{2,1,0:T(8,128)(2,1)S(1)} fusion(bf16[2,768,1280]{2,1,0:T(8,128)(2,1)} %collective-permute-done.1, bf16[1,768,1280]{2,1,0:T(8,128)(2,1)} %copy-done, bf16[1,768,1280]{2,1,0:T(8,128)(2,1)S(1)} %get-tuple-element.84, bf16[2,768,1280]{2,1,0:T(8,128)(2,1)} %collective-permute-done), kind=kLoop, calls=%fused_computation.23 | loop fusion | flops 47185920 | bytes 23592960 | tf_op jit(solution)/shard_map/concatenate | solution.py:42
  291.1 4.6 %fusion.28 = (bf16[1,2304,1280]{2,1,0:T(8,128)(2,1)}, bf16[1,2304,1280]{2,1,0:T(8,128)(2,1)}) fusion(bf16[2,2304,1280]{2,1,0:T(8,128)(2,1)S(1)} %pad_maximum_fusion), kind=kLoop, calls=%fused_computation.39 | loop fusion | bytes 23592960 | tf_op jit(solution)/shard_map/slice | solution.py:51
  295.6 8.8 %copy.29 = bf16[1,2304,1280]{1,2,0:T(8,128)(2,1)} copy(bf16[1,2304,1280]{2,1,0:T(8,128)(2,1)} %get-tuple-element.83) | data formatting | bytes 11796480 | tf_op jit(solution)/shard_map/slice | solution.py:50
  304.5 9.0 %copy.30 = bf16[1,2304,1280]{1,2,0:T(8,128)(2,1)} copy(bf16[1,2304,1280]{2,1,0:T(8,128)(2,1)} %get-tuple-element.82) | data formatting | bytes 11796480 | tf_op jit(solution)/shard_map/slice | solution.py:51
  313.5 88.0 %while.11 = (s32[]{:T(128)}, bf16[10,768,128]{1,2,0:T(8,128)(2,1)S(1)}, bf16[10,768,128]{1,2,0:T(8,128)(2,1)}, bf16[10,2304,128]{1,2,0:T(8,128)(2,1)}, bf16[10,2...) while((s32[]{:T(128)}, bf16[10,768,128]{1,2,0:T(8,128)(2,1)S(1)}, ...), condition=%wide.region_3.5_spmd.clone, body=%wide.region_0.4_spmd.clone.sunk | while | flops 918551040 | bytes 30692432 | solution.py:67
  314.0 1.9 copy.54
  315.9 2.9 fusion.36
  318.8 1.1 fusion.37
  319.9 2.3 fusion.38
  322.8 1.9 copy.54
  324.8 2.8 fusion.36
  327.6 1.1 fusion.37
  328.7 2.3 fusion.38
  331.6 1.9 copy.54
  333.5 2.8 fusion.36
  336.3 1.1 fusion.37
  337.4 2.3 fusion.38
  340.4 1.9 copy.54
  342.3 2.9 fusion.36
  345.2 1.1 fusion.37
  346.3 2.3 fusion.38
  349.2 1.9 copy.54
  351.1 2.8 fusion.36
  354.0 1.1 fusion.37
  355.1 2.3 fusion.38
  358.0 1.9 copy.54
  359.9 2.8 fusion.36
  362.7 1.1 fusion.37
  363.8 2.3 fusion.38
  366.8 1.9 copy.54
  368.7 2.9 fusion.36
  372.7 2.3 fusion.38
  375.6 1.9 copy.54
  377.5 2.8 fusion.36
  381.4 2.3 fusion.38
  384.4 1.9 copy.54
  386.3 2.8 fusion.36
  390.2 2.3 fusion.38
  393.1 1.9 copy.54
  395.1 2.9 fusion.36
  399.1 2.3 fusion.38
  401.5 2.3 copy.35
  403.8 7.1 %scatter_custom_fusion = bf16[768,1280]{1,0:T(8,128)(2,1)S(1)} fusion(s32[768]{0:T(1024)S(1)} %get-tuple-element.79, bf16[768,1280]{1,0:T(8,128)(2,1)} %copy.35, bf16[]{:T(256)} %constant.27.clone.1), kind=kCustom, calls=%fused_computation.31 | custom fusion | bytes 1966592 | tf_op jit(solution)/shard_map/scatter | solution.py:69
  410.9 26.8 %all_to_all.76 = bf16[4,192,1280]{2,1,0:T(8,128)(2,1)S(1)} all-to-all(bf16[4,192,1280]{2,1,0:T(8,128)(2,1)S(1)} %bitcast.78), channel_id=1, replica_groups=mesh['blk'=64,'head'=4] {'head'}, dimensions={0} | all-to-all | bytes 3932160 | tf_op jit(solution)/shard_map/all_to_all | solution.py:70
  437.7 1.5 copy.45
  (47 shorter events, 10.9 us)
Async XLA Ops:
  3.0 27.9 %all-to-all-start = ((bf16[192,4,1280]{2,0,1:T(8,128)(2,1)}), bf16[192,4,1280]{2,0,1:T(8,128)(2,1)S(1)}, u32[]{:S(2)}, u32[]{:S(2)}) async-start(bf16[192,4,1280]{2,0,1:T(8,128)(2,1)} %bitcast.77), calls=%async_computation | async-start | bytes 3932160 | tf_op jit(solution)/shard_map/all_to_all | solution.py:23
  30.8 28.8 %all-to-all-start.1 = ((bf16[192,4,1280]{2,0,1:T(8,128)(2,1)}), bf16[192,4,1280]{2,0,1:T(8,128)(2,1)}, u32[]{:S(2)}, u32[]{:S(2)}) async-start(bf16[192,4,1280]{2,0,1:T(8,128)(2,1)} %bitcast.76), calls=%async_computation.1 | async-start | bytes 3932160 | tf_op jit(solution)/shard_map/all_to_all | solution.py:24
  59.6 4.6 %copy-start.2 = (s32[768]{0:T(1024)S(1)}, s32[768]{0:T(1024)}, u32[]{:S(2)}) copy-start(s32[768]{0:T(1024)} %param.12) | copy-start | bytes 9220
  59.6 28.9 %all-to-all-start.2 = ((bf16[192,4,1280]{2,0,1:T(8,128)(2,1)}), bf16[192,4,1280]{2,0,1:T(8,128)(2,1)}, u32[]{:S(2)}, u32[]{:S(2)}) async-start(bf16[192,4,1280]{2,0,1:T(8,128)(2,1)} %bitcast.75), calls=%async_computation.2 | async-start | bytes 3932160 | tf_op jit(solution)/shard_map/all_to_all | solution.py:25
  100.1 2.5 copy-start
  100.1 11.0 %copy-start.3 = (s32[2,128]{1,0:T(2,128)S(1)}, s32[2,128]{1,0:T(2,128)}, u32[]{:S(2)}) copy-start(s32[2,128]{1,0:T(2,128)} %param.13) | copy-start | bytes 3076
  102.7 175.0 %collective-permute-start = (bf16[2,768,1280]{2,1,0:T(8,128)(2,1)}, bf16[2,768,1280]{2,1,0:T(8,128)(2,1)}, u32[]{:S(2)}, u32[]{:S(2)}) collective-permute-start(bf16[2,768,1280]{2,1,0:T(8,128)(2,1)} %pad_maximum_fusion.1), channel_id=1, source_target_pairs={{0,4},{4,8},{8,12},{12,16},{16,20},{20,24},{24,28},{28,32},{32,36}... | collective-permute-start | bytes 11796488 | tf_op jit(solution)/shard_map/ppermute | solution.py:14
  109.0 176.8 %collective-permute-start.1 = (bf16[2,768,1280]{2,1,0:T(8,128)(2,1)}, bf16[2,768,1280]{2,1,0:T(8,128)(2,1)}, u32[]{:S(2)}, u32[]{:S(2)}) collective-permute-start(bf16[2,768,1280]{2,1,0:T(8,128)(2,1)} %pad_maximum_fusion.1), channel_id=1, source_target_pairs={{4,0},{8,4},{12,8},{16,12},{20,16},{24,20},{28,24},{32,28},{36,32}... | collective-permute-start | bytes 11796488 | tf_op jit(solution)/shard_map/ppermute | solution.py:14
  304.5 9.1 %copy-start.1 = (bf16[10,768,128]{1,2,0:T(8,128)(2,1)S(1)}, bf16[10,768,128]{1,2,0:T(8,128)(2,1)}, u32[]{:S(2)}) copy-start(bf16[10,768,128]{1,2,0:T(8,128)(2,1)} %custom-call.6) | copy-start | bytes 5898244
where the time goes:
time: 441 us; the launch traced here: 439 us
  waiting for transfers between devices  227 us (51%)
  local copies, waits for them, and re-layouts  89.3 us (20%)
  matrix products  51.1 us (12%)
  blocking collectives  26.8 us (6%)
  other arithmetic  23.5 us (5%)
  starting transfers between devices  21 us (5%)
    ppermute x2, waiting for transfers between devices, from_behind(): return lax.ppermute(shard, axis, pairs)  171 us
    dot_general x10, matrix products, one_head(): jnp.einsum('qd,kd->qk', query_head, key_head, preferred_element_type=jnp....  28.5 us
    all_to_all x1, blocking collectives, local(): lax.all_to_all(raster, 'head', split_axis=0, concat_axis=1, tiled=True)  26.8 us
    dot_general x10, matrix products, one_head(): mixed = jnp.dot(rounded, value_head, preferred_element_type=jnp.float32)  22.7 us
    all_to_all x1, waiting for transfers between devices, local(): lax.all_to_all(key_input, 'head', split_axis=1, concat_axis=0, tiled=True)  21.4 us
    all_to_all x1, waiting for transfers between devices, local(): lax.all_to_all(queries, 'head', split_axis=1, concat_axis=0, tiled=True)  21.3 us
    reshape x10, local copies, waits for them, and re-layouts, local(): jnp.repeat(jnp.repeat(seen, tile_length, axis=0), tile_length, axis=1)  19.1 us
    all_to_all x1, waiting for transfers between devices, local(): lax.all_to_all(value_input, 'head', split_axis=1, concat_axis=0, tiled=True)  13.6 us
  transfers between devices with their start and end apart: 5, of which 5 were waited for; matrix products, arithmetic and copies ran while one was open for 5% of the time, Pallas kernels for 0%

commit v1 on v0

v1 whole, which is shorter than its diff:
```python
import functools
import math

import jax
import jax.numpy as jnp
from jax import lax
from jax.experimental import pallas as pl
from jax.experimental.pallas import tpu as pltpu
from jax.sharding import PartitionSpec as P

HEAD_DIM = 128
ROW = 4
PEERS = 2 * ROW
LANES = 128
HIDE = -(2.0**100)
MESH = pl.DeviceIdType.MESH


def kernel(
    heads, runs,
    q_in, k_in, v_in, order_ref, mask_ref,
    out,
    kbuf, vbuf, qbuf, obuf, info, km, qm, top_s, sum_s, acc_s,
    x_recv, x_send, z_recv, z_send, h_recv, h_send, o_recv, o_send, i_recv, i_send, ih_recv, ih_send,
):
    rows = q_in.shape[0]
    run_len = 4 * rows
    half = 2 * rows
    factor = math.log2(math.e) / math.sqrt(HEAD_DIM)

    blk = lax.axis_index("blk")
    head = lax.axis_index("head")
    x = lax.rem(blk, ROW)
    first = blk - x
    zl = lax.div(head, 2)
    core = lax.rem(head, 2)
    me = 2 * x + core
    quarter = head
    after = lax.rem(blk + ROW, runs)
    before = lax.rem(blk + runs - ROW, runs)
    halo_blk = lax.rem(blk + runs + (2 * zl - 1) * ROW, runs)
    halo_src = 1 + 3 * zl
    halo_dst = 5 - 5 * zl
    halo_side = 1 - zl

    def device(peer):
        return (first + lax.div(peer, 2), 2 * zl + lax.rem(peer, 2))

    partner = (blk, 2 * (1 - zl) + core)

    def peer_at(step):
        return lax.rem(me + step, PEERS)

    barrier = pltpu.get_barrier_semaphore()
    for step in range(1, PEERS):
        pl.semaphore_signal(barrier, inc=1, device_id=device(peer_at(step)), device_id_type=MESH)
    pl.semaphore_signal(barrier, inc=1, device_id=partner, device_id_type=MESH)
    pl.semaphore_signal(barrier, inc=1, device_id=(after, core), device_id_type=MESH)
    pl.semaphore_signal(barrier, inc=1, device_id=(before, 2 + core), device_id_type=MESH)
    pl.semaphore_wait(barrier, PEERS + 2)

    def columns(peer, j):
        return pl.ds(pl.multiple_of((heads * peer + j) * HEAD_DIM, HEAD_DIM), HEAD_DIM)

    def send(src, dst, send_sem, recv_sem, to):
        pltpu.make_async_remote_copy(
            src_ref=src, dst_ref=dst, send_sem=send_sem, recv_sem=recv_sem, device_id=to, device_id_type=MESH
        ).start()

    def wait(like, sem):
        pltpu.make_async_copy(like, like, sem).wait()

    def slab(buf, j):
        return buf.at[j, pl.ds(1, ROW), pl.ds(2 * zl, 2)]

    def partner_slab(buf, j):
        return buf.at[j, pl.ds(1, ROW), pl.ds(2 * (1 - zl), 2)]

    def x_start(j):
        for kind, (source, buf) in enumerate(((k_in, kbuf), (v_in, vbuf), (q_in, qbuf))):
            place = qbuf.at[j, me] if kind == 2 else buf.at[j, 1 + x, quarter]
            pltpu.make_async_copy(source.at[:, columns(me, j)], place, x_recv.at[kind, j]).start()
            for step in range(1, PEERS):
                peer = peer_at(step)
                send(
                    source.at[:, columns(peer, j)], place,
                    x_send.at[kind, j], x_recv.at[kind, j], device(peer),
                )

    x_start(0)

    order = (order_ref[...] - blk * run_len).astype(jnp.float32)
    order = jnp.transpose(jnp.broadcast_to(order, (LANES, run_len)))[half:]
    lane = lax.broadcasted_iota(jnp.int32, (half, LANES), 1).astype(jnp.float32)
    second = jnp.concatenate(
        [
            jnp.sum(jnp.where(order == lane + LANES * g, 1.0, 0.0), axis=0, keepdims=True)
            for g in range(run_len // LANES)
        ],
        axis=1,
    )
    seen = mask_ref[...].astype(jnp.float32)
    mask_lane = lax.broadcasted_iota(jnp.int32, seen.shape, 1)

    def bias(offset):
        column = jnp.sum(jnp.where(mask_lane == 2 * blk + offset, seen, 0.0), axis=1, keepdims=True)
        return HIDE * (1.0 - (column[0:1] + second * (column[1:2] - column[0:1])))

    which = lax.broadcasted_iota(jnp.int32, (16, run_len), 0)

    def stack(parts):
        total = jnp.zeros((16, run_len), jnp.float32)
        for index, part in enumerate(parts):
            total = jnp.where(which == index, part, total)
        return total.astype(jnp.bfloat16)

    mine = info.at[1 + x]
    mine[0:16] = stack((1.0 - second, second, 1.0 - second, second))
    mine[16:32] = stack((bias(-2), bias(-1), bias(2), bias(3)))
    for step in range(1, ROW):
        to = (first + lax.rem(x + step, ROW), head)
        send(mine, mine, i_send, i_recv, to)

    def spread(values):
        tall = jnp.concatenate([values, jnp.zeros((LANES - 16, run_len), jnp.float32)], axis=0)
        return jnp.transpose(tall).astype(jnp.bfloat16)

    def key_marks(slot):
        km[slot] = spread(info[slot, 0:16].astype(jnp.float32))

    def halo_start(kind, buf, j):
        for target in range(2):
            send(
                buf.at[j, halo_src], buf.at[j, halo_dst],
                h_send.at[kind, j], h_recv.at[halo_side, kind, j], (halo_blk, 2 * target + core),
            )

    def query(j, r):
        return qbuf[j, pl.ds(2 * r, 2)].reshape(half, HEAD_DIM)

    def add_run(state, j, r, slot, side):
        top, total, acc = state
        q = query(j, r)
        k = kbuf[j, slot].reshape(run_len, HEAD_DIM)
        v = vbuf[j, slot].reshape(run_len, HEAD_DIM)
        if side is not None:
            marks = qm[side, r, pl.ds(pl.multiple_of(zl * half, half), half)]
            q = jnp.concatenate([q, marks], axis=1)
            k = jnp.concatenate([k, km[slot]], axis=1)
        scores = lax.dot_general(q, k, (((1,), (1,)), ((), ())), preferred_element_type=jnp.float32) * factor
        high = jnp.max(scores, axis=1, keepdims=True)
        new = high if top is None else jnp.maximum(top, high)
        weights = jnp.exp2(scores - new)
        part = jnp.sum(weights, axis=1, keepdims=True)
        mixed = jnp.dot(weights.astype(jnp.bfloat16), v, preferred_element_type=jnp.float32)
        if top is None:
            return new, part, mixed
        fade = jnp.exp2(top - new)
        return new, total * fade + part, acc * fade + mixed

    def finish(state, j, r):
        _, total, acc = state
        obuf[j, pl.ds(2 * r, 2)] = (acc / total).astype(jnp.bfloat16).reshape(2, rows, HEAD_DIM)

    def send_out(j, peers):
        for peer in peers:
            @pl.when(peer != me)
            def _():
                send(obuf.at[j, peer], out.at[:, columns(me, j)], o_send.at[j], o_recv, device(peer))

            @pl.when(peer == me)
            def _():
                pltpu.make_async_copy(obuf.at[j, peer], out.at[:, columns(me, j)], o_recv).start()

    def keep(state, edge):
        top, total, acc = state
        top_s[edge] = jnp.broadcast_to(top, (half, LANES))
        sum_s[edge] = jnp.broadcast_to(total, (half, LANES))
        acc_s[edge] = acc

    def kept(edge):
        return top_s[edge][:, 0:1], sum_s[edge][:, 0:1], acc_s[edge]

    nothing = (None, None, None)

    def inner(j):
        keep(add_run(add_run(nothing, j, 0, 1, None), j, 0, 2, 1), 0)
        keep(add_run(add_run(nothing, j, 3, 4, None), j, 3, 3, 0), 1)

        def middle(r, carry):
            state = add_run(nothing, j, r, r + 1, None)
            state = add_run(state, j, r, r, 0)
            state = add_run(state, j, r, r + 2, 1)
            finish(state, j, r)
            return carry

        lax.fori_loop(1, 3, middle, 0)
        send_out(j, [2 + lax.rem(me + step, 4) for step in range(4)])

    def edges(j):
        finish(add_run(kept(0), j, 0, 0, 0), j, 0)
        finish(add_run(kept(1), j, 3, 5, 1), j, 3)
        send_out(j, [lax.rem(6 + lax.rem(me + step, 4), PEERS) for step in range(4)])

    def one_head(j, carry):
        @pl.when(j < heads)
        def _():
            for kind, buf in enumerate((kbuf, vbuf)):
                wait(slab(buf, j), x_recv.at[kind, j])
                send(slab(buf, j), slab(buf, j), z_send.at[kind, j], z_recv.at[kind, j], partner)

        @pl.when(j + 1 < heads)
        def _():
            x_start(j + 1)

        @pl.when(j == 0)
        def _():
            wait(info.at[pl.ds(0, ROW - 1)], i_recv)
            for target in range(2):
                send(
                    info.at[halo_src], info.at[halo_dst],
                    ih_send, ih_recv.at[halo_side], (halo_blk, 2 * target + core),
                )
            for r in range(ROW):
                key_marks(1 + r)
                marks = info[1 + r, 16:32].astype(jnp.float32)
                qm[0, r] = spread(jnp.where(which < 2, marks, 0.0))
                qm[1, r] = spread(jnp.where(which >= 2, marks, 0.0))

        @pl.when(j > 0)
        def _():
            @pl.when(j == 1)
            def _():
                wait(info.at[0], ih_recv.at[0])
                wait(info.at[5], ih_recv.at[1])
                key_marks(0)
                key_marks(5)

            for side, slot in ((0, 0), (1, 5)):
                for kind, buf in enumerate((kbuf, vbuf)):
                    wait(buf.at[j - 1, slot], h_recv.at[side, kind, j - 1])
            edges(j - 1)

        @pl.when(j < heads)
        def _():
            for kind, buf in enumerate((kbuf, vbuf)):
                wait(partner_slab(buf, j), z_recv.at[kind, j])
                halo_start(kind, buf, j)
            wait(qbuf.at[j], x_recv.at[2, j])
            inner(j)

        return carry

    lax.fori_loop(0, heads + 1, one_head, 0)

    wait(out, o_recv)
    wait(info.at[pl.ds(0, ROW - 1)], i_send)
    wait(info.at[pl.ds(0, 2)], ih_send)

    def drain(j, carry):
        for kind, buf in enumerate((kbuf, vbuf, qbuf)):
            wait(qbuf.at[j, pl.ds(0, PEERS - 1)], x_send.at[kind, j])
            if kind < 2:
                wait(slab(buf, j), z_send.at[kind, j])
                wait(buf.at[j, pl.ds(0, 2)], h_send.at[kind, j])
        wait(qbuf.at[j, pl.ds(0, PEERS - 1)], o_send.at[j])
        return carry

    lax.fori_loop(0, heads, drain, 0)


def local(queries, key_input, value_input, token_order, tile_mask):
    rows, width = queries.shape
    heads = width // HEAD_DIM // PEERS
    runs = lax.axis_size("blk")
    run_len = 4 * rows
    half = 2 * rows
    bf16, f32 = jnp.bfloat16, jnp.float32
    dma = pltpu.SemaphoreType.DMA
    hbm = pl.BlockSpec(memory_space=pl.ANY)
    vmem = pl.BlockSpec(memory_space=pltpu.VMEM)
    flops = 4 * heads * ROW * half * 3 * run_len * HEAD_DIM
    return pl.pallas_call(
        functools.partial(kernel, heads, runs),
        out_shape=jax.ShapeDtypeStruct(queries.shape, queries.dtype),
        in_specs=[hbm, hbm, hbm, vmem, vmem],
        out_specs=hbm,
        scratch_shapes=[
            pltpu.VMEM((heads, 6, 4, rows, HEAD_DIM), bf16),
            pltpu.VMEM((heads, 6, 4, rows, HEAD_DIM), bf16),
            pltpu.VMEM((heads, PEERS, rows, HEAD_DIM), bf16),
            pltpu.VMEM((heads, PEERS, rows, HEAD_DIM), bf16),
            pltpu.VMEM((6, 32, run_len), bf16),
            pltpu.VMEM((6, run_len, LANES), bf16),
            pltpu.VMEM((2, ROW, run_len, LANES), bf16),
            pltpu.VMEM((2, half, LANES), f32),
            pltpu.VMEM((2, half, LANES), f32),
            pltpu.VMEM((2, half, HEAD_DIM), f32),
            dma((3, heads)), dma((3, heads)),
            dma((2, heads)), dma((2, heads)),
            dma((2, 2, heads)), dma((2, heads)),
            dma, dma((heads,)),
            dma, dma,
            dma((2,)), dma,
        ],
        compiler_params=pltpu.CompilerParams(
            collective_id=0, has_side_effects=True, vmem_limit_bytes=56 * 1024 * 1024
        ),
        cost_estimate=pl.CostEstimate(
            flops=flops, bytes_accessed=8 * rows * width, transcendentals=flops // (4 * HEAD_DIM)
        ),
    )(queries, key_input, value_input, token_order.reshape(1, run_len), tile_mask)


def solution(mesh):
    in_specs = (
        P(("blk", "head"), None),
        P(("blk", "head"), None),
        P(("blk", "head"), None),
        P("blk"),
        P("blk", None),
    )
    out_specs = P(("blk", "head"), None)
    return jax.shard_map(local, mesh=mesh, in_specs=in_specs, out_specs=out_specs, check_vma=False)
```

time: 441 us -> 196 us (0.44)
  the two profiles are of different devices: /device:TPU:78 before, /device:TPU:33 now
where the time goes in v1:
time: 196 us; the launch traced here: 194 us
  Pallas kernels  190 us (97%)
  local copies, waits for them, and re-layouts  4.21 us (2%)
    pallas_call x1, Pallas kernels, local(): pl.pallas_call(functools.partial(kernel, heads, runs), out_shape=jax.Shap...  190 us

profile of v1, /device:TPU:33, one launch (start us, length us, event | category | flops | bytes accessed | tf_op | source)
XLA Modules:
  0.0 193.8 jit_solution(2751575481857622793)
XLA Ops:
  0.0 1.3 reshape.3.order_ref
  1.3 189.6 %shard_map.55 = bf16[192,5120]{1,0:T(8,128)(2,1)} custom-call(bf16[192,5120]{1,0:T(8,128)(2,1)} %q_in.1, bf16[192,5120]{1,0:T(8,128)(2,1)} %k_in.1, bf16[192,5120]{1,0:T(8,128)(2,1)} %v_in.1, s32[1,768]{1,0:T(1,128)} %reshape.3.order_ref, s32[2,128]{1,0:T(2,128)} %mask_ref.1), custom_call_target="tpu_custom_call" | custom-call | flops 9059696640 | bytes 7864320 | tf_op jit(solution)/shard_map/pallas_call | solution.py:283
  190.8 2.9 %copy.7 = bf16[192,5120]{1,0:T(8,128)(2,1)} copy(bf16[192,5120]{1,0:T(8,128)(2,1)} %shard_map.55) | data formatting | bytes 3932160

commit v2 on v1

v2 whole, which is shorter than its diff:
```python
import functools
import math

import jax
import jax.numpy as jnp
from jax import lax
from jax.experimental import pallas as pl
from jax.experimental.pallas import tpu as pltpu
from jax.sharding import PartitionSpec as P

HEAD_DIM = 128
ROW = 4
PEERS = 2 * ROW
LANES = 128
HIDE = -(2.0**100)
MESH = pl.DeviceIdType.MESH


def kernel(
    heads, runs,
    q_in, k_in, v_in, order_ref, mask_ref,
    out,
    kbuf, vbuf, qbuf, obuf, q_far, o_far, o_back, log_far, log_back, info, km, qm, top_s, sum_s, acc_s,
    x_recv, x_send, z_recv, z_send, d_send, h_recv, h_send, o_recv, o_send, i_recv, i_send, ih_recv, ih_send,
    q_recv, q_send, p_recv, p_send, l_recv, l_send,
):
    rows = q_in.shape[0]
    run_len = 4 * rows
    half = 2 * rows
    factor = math.log2(math.e) / math.sqrt(HEAD_DIM)
    last = ROW - 1

    blk = lax.axis_index("blk")
    head = lax.axis_index("head")
    x = lax.rem(blk, ROW)
    first = blk - x
    zl = lax.div(head, 2)
    core = lax.rem(head, 2)
    me = 2 * x + core
    across = 2 * (1 - zl)
    partner = (blk, across + core)
    mate = (lax.rem(blk + runs + (2 * zl - 1) * ROW, runs), across + core)
    own_edge = last * zl
    far_edge = last * (1 - zl)

    def device(peer):
        return (first + lax.div(peer, 2), 2 * zl + lax.rem(peer, 2))

    def peer_at(step):
        return lax.rem(me + step, PEERS)

    barrier = pltpu.get_barrier_semaphore()
    greet = [device(peer_at(step)) for step in range(1, PEERS)]
    greet += [partner, (blk, across + 1 - core), mate]
    for to in greet:
        pl.semaphore_signal(barrier, inc=1, device_id=to, device_id_type=MESH)
    pl.semaphore_wait(barrier, len(greet))

    def columns(peer, j):
        return pl.ds(pl.multiple_of((heads * peer + j) * HEAD_DIM, HEAD_DIM), HEAD_DIM)

    def send(src, dst, send_sem, recv_sem, to):
        pltpu.make_async_remote_copy(
            src_ref=src, dst_ref=dst, send_sem=send_sem, recv_sem=recv_sem, device_id=to, device_id_type=MESH
        ).start()

    def wait(like, sem):
        pltpu.make_async_copy(like, like, sem).wait()

    sources = ((0, k_in, kbuf), (1, v_in, vbuf), (2, q_in, qbuf))

    def direct_start(j):
        for kind, source, buf in sources[:2]:
            for c in range(2):
                send(
                    source.at[:, columns(2 * x + c, j)], buf.at[j, x, head],
                    d_send.at[kind, j], z_recv.at[kind, j, x], (blk, across + c),
                )

    def x_start(j):
        for kind, source, buf in sources:
            place = qbuf.at[j, me] if kind == 2 else buf.at[j, x, head]
            pltpu.make_async_copy(source.at[:, columns(me, j)], place, x_recv.at[kind, j, x]).start()
            for step in range(1, PEERS):
                peer = peer_at(step)
                send(
                    source.at[:, columns(peer, j)], place,
                    x_send.at[kind, j], x_recv.at[kind, j, x], device(peer),
                )

    def unit(buf, j, run, side):
        return buf.at[j, run, pl.ds(2 * side, 2)]

    def z_start(j, run):
        for kind, _, buf in sources[:2]:
            wait(unit(buf, j, run, zl), x_recv.at[kind, j, run])

            @pl.when(run != x)
            def _():
                send(
                    unit(buf, j, run, zl), unit(buf, j, run, zl),
                    z_send.at[kind, j, run], z_recv.at[kind, j, run], partner,
                )

    def queries_of(j, run):
        return qbuf.at[j, pl.ds(2 * run, 2)]

    def q_start(j):
        for run in range(ROW):
            wait(queries_of(j, run), x_recv.at[2, j, run])
        send(queries_of(j, far_edge), q_far.at[j], q_send.at[j], q_recv.at[j], partner)

    direct_start(0)
    x_start(0)
    for j in range(1, heads):
        direct_start(j)

    order = (order_ref[...] - blk * run_len).astype(jnp.float32)
    order = jnp.transpose(jnp.broadcast_to(order, (LANES, run_len)))[half:]
    lane = lax.broadcasted_iota(jnp.int32, (half, LANES), 1).astype(jnp.float32)
    second = jnp.concatenate(
        [
            jnp.sum(jnp.where(order == lane + LANES * g, 1.0, 0.0), axis=0, keepdims=True)
            for g in range(run_len // LANES)
        ],
        axis=1,
    )
    seen = mask_ref[...].astype(jnp.float32)
    mask_lane = lax.broadcasted_iota(jnp.int32, seen.shape, 1)

    def bias(offset):
        column = jnp.sum(jnp.where(mask_lane == 2 * blk + offset, seen, 0.0), axis=1, keepdims=True)
        return HIDE * (1.0 - (column[0:1] + second * (column[1:2] - column[0:1])))

    which = lax.broadcasted_iota(jnp.int32, (16, run_len), 0)

    def stack(parts):
        total = jnp.zeros((16, run_len), jnp.float32)
        for index, part in enumerate(parts):
            total = jnp.where(which == index, part, total)
        return total.astype(jnp.bfloat16)

    mine = info.at[x]
    mine[0:16] = stack((1.0 - second, second, 1.0 - second, second))
    mine[16:32] = stack((bias(-2), bias(-1), bias(2), bias(3)))
    for step in range(1, ROW):
        send(mine, mine, i_send, i_recv, (first + lax.rem(x + step, ROW), head))

    def spread(values):
        tall = jnp.concatenate([values, jnp.zeros((LANES - 16, run_len), jnp.float32)], axis=0)
        return jnp.transpose(tall).astype(jnp.bfloat16)

    def key_marks(slot):
        km[slot] = spread(info[slot, 0:16].astype(jnp.float32))

    def add_keys(state, q, marks, j, slot):
        top, total, acc = state
        k = kbuf[j, slot].reshape(run_len, HEAD_DIM)
        v = vbuf[j, slot].reshape(run_len, HEAD_DIM)
        if marks is not None:
            q = jnp.concatenate([q, marks], axis=1)
            k = jnp.concatenate([k, km[slot]], axis=1)
        scores = lax.dot_general(q, k, (((1,), (1,)), ((), ())), preferred_element_type=jnp.float32) * factor
        high = jnp.max(scores, axis=1, keepdims=True)
        new = high if top is None else jnp.maximum(top, high)
        weights = jnp.exp2(scores - new)
        part = jnp.sum(weights, axis=1, keepdims=True)
        mixed = jnp.dot(weights.astype(jnp.bfloat16), v, preferred_element_type=jnp.float32)
        if top is None:
            return new, part, mixed
        fade = jnp.exp2(top - new)
        return new, total * fade + part, acc * fade + mixed

    def load(j, run):
        at = lax.rem(j, 2)
        return top_s[at, run][:, 0:1], sum_s[at, run][:, 0:1], acc_s[at, run]

    def store(state, j, run):
        at = lax.rem(j, 2)
        top, total, acc = state
        top_s[at, run] = jnp.broadcast_to(top, (half, LANES))
        sum_s[at, run] = jnp.broadcast_to(total, (half, LANES))
        acc_s[at, run] = acc

    def marks_of(side, run, of):
        return qm[side, run, pl.ds(pl.multiple_of(of * half, half), half)]

    def my_queries(j, run):
        return queries_of(j, run)[...].reshape(half, HEAD_DIM)

    def step(j, run, slot, side):
        marks = None if side is None else marks_of(side, run, zl)
        store(add_keys(load(j, run), my_queries(j, run), marks, j, slot), j, run)

    def finish(acc, total, j, run):
        queries_like = (acc / total).astype(jnp.bfloat16).reshape(2, rows, HEAD_DIM)
        obuf[j, pl.ds(2 * run, 2)] = queries_like
        for c in range(2):
            peer = 2 * run + c

            @pl.when(peer != me)
            def _():
                send(obuf.at[j, peer], out.at[:, columns(me, j)], o_send.at[j], o_recv, device(peer))

            @pl.when(peer == me)
            def _():
                pltpu.make_async_copy(obuf.at[j, peer], out.at[:, columns(me, j)], o_recv).start()

    def finish_run(j, run):
        _, total, acc = load(j, run)
        finish(acc, total, j, run)

    def outer(j):
        @pl.when(j == 0)
        def _():
            wait(info.at[ROW], ih_recv)
            key_marks(ROW)

        for kind, _, buf in sources[:2]:
            wait(buf.at[j, ROW], h_recv.at[kind, j])
        wait(q_far.at[j], q_recv.at[j])
        far = q_far[j].reshape(half, HEAD_DIM)
        top, total, acc = add_keys((None, None, None), far, marks_of(zl, own_edge, 1 - zl), j, ROW)
        o_far[j] = (acc / total).astype(jnp.bfloat16).reshape(2, rows, HEAD_DIM)
        logs = jnp.broadcast_to(top + jnp.log2(total), (half, LANES))
        log_far[j] = jnp.transpose(logs)[0:8]
        send(o_far.at[j], o_back.at[j], p_send.at[j], p_recv.at[j], partner)
        send(log_far.at[j], log_back.at[j], l_send.at[j], l_recv.at[j], partner)
        state = add_keys(load(j, own_edge), my_queries(j, own_edge), marks_of(zl, own_edge, zl), j, ROW)
        finish(state[2], state[1], j, own_edge)

    def merge(j):
        wait(o_back.at[j], p_recv.at[j])
        wait(log_back.at[j], l_recv.at[j])
        top, total, acc = load(j, far_edge)
        logs = jnp.concatenate([log_back[j], jnp.zeros((LANES - 8, half), jnp.float32)], axis=0)
        log = jnp.transpose(logs)[:, 0:1]
        high = jnp.maximum(top, log)
        fade, other = jnp.exp2(top - high), jnp.exp2(log - high)
        back = o_back[j].reshape(half, HEAD_DIM).astype(jnp.float32)
        finish(acc * fade + back * other, total * fade + other, j, far_edge)

    def mirrored(index, flip):
        return index + flip * (last - 2 * index)

    def send_ahead(j, index):
        z_start(j, mirrored(index, 1 - zl))

        @pl.when(index == 1)
        def _():
            @pl.when(j + 1 < heads)
            def _():
                x_start(j + 1)

        @pl.when(index == last)
        def _():
            q_start(j)

    def ahead_first(index, carry):
        send_ahead(0, index)
        return carry

    lax.fori_loop(0, ROW, ahead_first, 0)

    def one_unit(t, carry):
        j = lax.div(t, ROW)
        index = lax.rem(t, ROW)
        run = mirrored(index, zl)

        @pl.when(j + 1 < heads)
        def _():
            send_ahead(j + 1, index)

        @pl.when(t == 0)
        def _():
            wait(info.at[pl.ds(0, ROW - 1)], i_recv)
            send(info.at[own_edge], info.at[ROW], ih_send, ih_recv, mate)
            for r in range(ROW):
                key_marks(r)
                marks = info[r, 16:32].astype(jnp.float32)
                qm[0, r] = spread(jnp.where(which < 2, marks, 0.0))
                qm[1, r] = spread(jnp.where(which >= 2, marks, 0.0))

        @pl.when(index == 0)
        def _():
            at = lax.rem(j, 2)
            top_s[at] = jnp.full((ROW, half, LANES), 4.0 * HIDE, jnp.float32)
            sum_s[at] = jnp.zeros((ROW, half, LANES), jnp.float32)
            acc_s[at] = jnp.zeros((ROW, half, HEAD_DIM), jnp.float32)

        @pl.when((index == 2) & (j > 0))
        def _():
            merge(j - 1)

        @pl.when(index == last)
        def _():
            outer(j)

        for kind, _, buf in sources[:2]:
            wait(unit(buf, j, run, 1 - zl), z_recv.at[kind, j, run])

        @pl.when(index == 0)
        def _():
            for kind, _, buf in sources[:2]:
                send(buf.at[j, run], buf.at[j, ROW], h_send.at[kind, j], h_recv.at[kind, j], mate)

        step(j, run, run, None)

        @pl.when(run < last)
        def _():
            step(j, run + 1, run, 0)

        @pl.when(run > 0)
        def _():
            step(j, run - 1, run, 1)

        @pl.when(index >= 2)
        def _():
            finish_run(j, mirrored(index - 1, zl))

        return carry

    lax.fori_loop(0, heads * ROW, one_unit, 0)
    merge(heads - 1)

    wait(out, o_recv)
    wait(info.at[pl.ds(0, ROW - 1)], i_send)
    wait(info.at[0], ih_send)

    def drain(j, carry):
        for kind, _, buf in sources:
            wait(qbuf.at[j, pl.ds(0, PEERS - 1)], x_send.at[kind, j])
            if kind < 2:
                wait(qbuf.at[j, pl.ds(0, 2)], d_send.at[kind, j])
                wait(buf.at[j, ROW], h_send.at[kind, j])
                for run in range(ROW):
                    @pl.when(run != x)
                    def _():
                        wait(unit(buf, j, run, zl), z_send.at[kind, j, run])
        wait(qbuf.at[j, pl.ds(0, PEERS - 1)], o_send.at[j])
        wait(q_far.at[j], q_send.at[j])
        wait(o_far.at[j], p_send.at[j])
        wait(log_far.at[j], l_send.at[j])
        return carry

    lax.fori_loop(0, heads, drain, 0)


def local(queries, key_input, value_input, token_order, tile_mask):
    rows, width = queries.shape
    heads = width // HEAD_DIM // PEERS
    runs = lax.axis_size("blk")
    run_len = 4 * rows
    half = 2 * rows
    bf16, f32 = jnp.bfloat16, jnp.float32
    dma = pltpu.SemaphoreType.DMA
    hbm = pl.BlockSpec(memory_space=pl.ANY)
    vmem = pl.BlockSpec(memory_space=pltpu.VMEM)
    flops = 4 * heads * ROW * half * 3 * run_len * HEAD_DIM
    return pl.pallas_call(
        functools.partial(kernel, heads, runs),
        out_shape=jax.ShapeDtypeStruct(queries.shape, queries.dtype),
        in_specs=[hbm, hbm, hbm, vmem, vmem],
        out_specs=hbm,
        scratch_shapes=[
            pltpu.VMEM((heads, ROW + 1, 4, rows, HEAD_DIM), bf16),
            pltpu.VMEM((heads, ROW + 1, 4, rows, HEAD_DIM), bf16),
            pltpu.VMEM((heads, PEERS, rows, HEAD_DIM), bf16),
            pltpu.VMEM((heads, PEERS, rows, HEAD_DIM), bf16),
            pltpu.VMEM((heads, 2, rows, HEAD_DIM), bf16),
            pltpu.VMEM((heads, 2, rows, HEAD_DIM), bf16),
            pltpu.VMEM((heads, 2, rows, HEAD_DIM), bf16),
            pltpu.VMEM((heads, 8, half), f32),
            pltpu.VMEM((heads, 8, half), f32),
            pltpu.VMEM((ROW + 1, 32, run_len), bf16),
            pltpu.VMEM((ROW + 1, run_len, LANES), bf16),
            pltpu.VMEM((2, ROW, run_len, LANES), bf16),
            pltpu.VMEM((2, ROW, half, LANES), f32),
            pltpu.VMEM((2, ROW, half, LANES), f32),
            pltpu.VMEM((2, ROW, half, HEAD_DIM), f32),
            dma((3, heads, ROW)), dma((3, heads)),
            dma((2, heads, ROW)), dma((2, heads, ROW)), dma((2, heads)),
            dma((2, heads)), dma((2, heads)),
            dma, dma((heads,)),
            dma, dma, dma, dma,
            dma((heads,)), dma((heads,)),
            dma((heads,)), dma((heads,)),
            dma((heads,)), dma((heads,)),
        ],
        compiler_params=pltpu.CompilerParams(
            collective_id=0, has_side_effects=True, vmem_limit_bytes=56 * 1024 * 1024
        ),
        cost_estimate=pl.CostEstimate(
            flops=flops, bytes_accessed=8 * rows * width, transcendentals=flops // (4 * HEAD_DIM)
        ),
    )(queries, key_input, value_input, token_order.reshape(1, run_len), tile_mask)


def solution(mesh):
    in_specs = (
        P(("blk", "head"), None),
        P(("blk", "head"), None),
        P(("blk", "head"), None),
        P("blk"),
        P("blk", None),
    )
    out_specs = P(("blk", "head"), None)
    return jax.shard_map(local, mesh=mesh, in_specs=in_specs, out_specs=out_specs, check_vma=False)
```

time: 196 us -> 137 us (0.70)
  Pallas kernels: 190 us -> 132 us
    pallas_call x1, Pallas kernels: 190 us -> 132 us  [local(): pl.pallas_call(functools.partial(kernel, heads, runs), out_shape=jax.Shap...]
where the time goes in v2:
time: 137 us
  Pallas kernels  132 us (96%)
  local copies, waits for them, and re-layouts  4.21 us (3%)
    pallas_call x1, Pallas kernels, local(): pl.pallas_call(functools.partial(kernel, heads, runs), out_shape=jax.Shap...  132 us
    unnamed x1, local copies, waits for them, and re-layouts  2.94 us

profile of v2, /device:TPU:33, one launch (start us, length us, event | category | flops | bytes accessed | tf_op | source)
XLA Modules:
  0.0 136.6 jit_solution(7855118762698674247)
XLA Ops:
  0.0 1.3 reshape.3.order_ref
  1.3 132.4 %shard_map.55 = bf16[192,5120]{1,0:T(8,128)(2,1)} custom-call(bf16[192,5120]{1,0:T(8,128)(2,1)} %q_in.1, bf16[192,5120]{1,0:T(8,128)(2,1)} %k_in.1, bf16[192,5120]{1,0:T(8,128)(2,1)} %v_in.1, s32[1,768]{1,0:T(1,128)} %reshape.3.order_ref, s32[2,128]{1,0:T(2,128)} %mask_ref.1), custom_call_target="tpu_custom_call" | custom-call | flops 9059696640 | bytes 7864320 | tf_op jit(solution)/shard_map/pallas_call | solution.py:360
  133.7 2.9 %copy.7 = bf16[192,5120]{1,0:T(8,128)(2,1)} copy(bf16[192,5120]{1,0:T(8,128)(2,1)} %shard_map.55) | data formatting | bytes 3932160

commit v3 on v2

v3 whole, which is shorter than its diff:
```python
import functools
import math

import jax
import jax.numpy as jnp
from jax import lax
from jax.experimental import pallas as pl
from jax.experimental.pallas import tpu as pltpu
from jax.sharding import PartitionSpec as P

HEAD_DIM = 128
ROW = 4
PEERS = 2 * ROW
LANES = 128
HIDE = -(2.0**100)
MESH = pl.DeviceIdType.MESH


def kernel(
    heads, runs,
    q_in, k_in, v_in, order_ref, mask_ref,
    out,
    kbuf, vbuf, qbuf, obuf, q_far, o_far, o_back, log_far, log_back, info, km, qm, top_s, sum_s, acc_s,
    x_recv, x_send, z_recv, z_send, d_send, h_recv, h_send, o_recv, o_send, i_recv, i_send, ih_recv, ih_send,
    q_recv, q_send, p_recv, p_send, l_recv, l_send,
):
    rows = q_in.shape[0]
    run_len = 4 * rows
    half = 2 * rows
    factor = math.log2(math.e) / math.sqrt(HEAD_DIM)
    last = ROW - 1

    blk = lax.axis_index("blk")
    head = lax.axis_index("head")
    x = lax.rem(blk, ROW)
    first = blk - x
    zl = lax.div(head, 2)
    core = lax.rem(head, 2)
    me = 2 * x + core
    across = 2 * (1 - zl)
    partner = (blk, across + core)
    mate = (lax.rem(blk + runs + (2 * zl - 1) * ROW, runs), across + core)
    own_edge = last * zl
    far_edge = last * (1 - zl)

    def device(peer):
        return (first + lax.div(peer, 2), 2 * zl + lax.rem(peer, 2))

    def peer_at(step):
        return lax.rem(me + step, PEERS)

    barrier = pltpu.get_barrier_semaphore()
    greet = [device(peer_at(step)) for step in range(1, PEERS)]
    greet += [partner, (blk, across + 1 - core), mate]
    for to in greet:
        pl.semaphore_signal(barrier, inc=1, device_id=to, device_id_type=MESH)

    order = (order_ref[...].reshape(1, run_len) - blk * run_len).astype(jnp.float32)
    order = jnp.transpose(jnp.broadcast_to(order, (LANES, run_len)))[half:]
    lane = lax.broadcasted_iota(jnp.int32, (half, LANES), 1).astype(jnp.float32)
    second = jnp.concatenate(
        [
            jnp.sum(jnp.where(order == lane + LANES * g, 1.0, 0.0), axis=0, keepdims=True)
            for g in range(run_len // LANES)
        ],
        axis=1,
    )
    seen = mask_ref[...].astype(jnp.float32)
    mask_lane = lax.broadcasted_iota(jnp.int32, seen.shape, 1)

    def bias(offset):
        column = jnp.sum(jnp.where(mask_lane == 2 * blk + offset, seen, 0.0), axis=1, keepdims=True)
        return HIDE * (1.0 - (column[0:1] + second * (column[1:2] - column[0:1])))

    which = lax.broadcasted_iota(jnp.int32, (16, run_len), 0)
    log_row = lax.broadcasted_iota(jnp.int32, (8, LANES), 0)

    def stack(parts):
        total = jnp.zeros((16, run_len), jnp.float32)
        for index, part in enumerate(parts):
            total = jnp.where(which == index, part, total)
        return total.astype(jnp.bfloat16)

    mine = info.at[x]
    mine[0:16] = stack((1.0 - second, second, 1.0 - second, second))
    mine[16:32] = stack((bias(-2), bias(-1), bias(2), bias(3)))
    pl.semaphore_wait(barrier, len(greet))

    def columns(peer, j):
        return pl.ds(pl.multiple_of((heads * peer + j) * HEAD_DIM, HEAD_DIM), HEAD_DIM)

    def send(src, dst, send_sem, recv_sem, to):
        pltpu.make_async_remote_copy(
            src_ref=src, dst_ref=dst, send_sem=send_sem, recv_sem=recv_sem, device_id=to, device_id_type=MESH
        ).start()

    def wait(like, sem):
        pltpu.make_async_copy(like, like, sem).wait()

    sources = ((0, k_in, kbuf), (1, v_in, vbuf), (2, q_in, qbuf))

    def direct_start(j):
        for kind, source, buf in sources[:2]:
            for c in range(2):
                send(
                    source.at[:, columns(2 * x + c, j)], buf.at[j, x, head],
                    d_send.at[kind, j], z_recv.at[kind, j, x], (blk, across + c),
                )

    def x_start(j):
        for kind, source, buf in sources:
            place = qbuf.at[j, me] if kind == 2 else buf.at[j, x, head]
            pltpu.make_async_copy(source.at[:, columns(me, j)], place, x_recv.at[kind, j, x]).start()
            for step in range(1, PEERS):
                peer = peer_at(step)
                send(
                    source.at[:, columns(peer, j)], place,
                    x_send.at[kind, j], x_recv.at[kind, j, x], device(peer),
                )

    def unit(buf, j, run, side):
        return buf.at[j, run, pl.ds(2 * side, 2)]

    def halo_start(kind, buf, j, side):
        send(unit(buf, j, own_edge, side), unit(buf, j, ROW, side), h_send.at[kind, j], h_recv.at[kind, j], mate)

    def z_start(j, run):
        for kind, _, buf in sources[:2]:
            wait(unit(buf, j, run, zl), x_recv.at[kind, j, run])

            @pl.when((run != x) | (j == heads - 1))
            def _():
                send(
                    unit(buf, j, run, zl), unit(buf, j, run, zl),
                    z_send.at[kind, j], z_recv.at[kind, j, run], partner,
                )

            @pl.when(run == own_edge)
            def _():
                halo_start(kind, buf, j, zl)

    def queries_of(j, run):
        return qbuf.at[j, pl.ds(2 * run, 2)]

    def q_start(j):
        for run in range(ROW):
            wait(queries_of(j, run), x_recv.at[2, j, run])
        send(queries_of(j, far_edge), q_far.at[j], q_send.at[j], q_recv.at[j], partner)

    direct_start(0)
    x_start(0)
    for j in range(1, heads - 1):
        direct_start(j)

    for step in range(1, ROW):
        send(mine, mine, i_send, i_recv, (first + lax.rem(x + step, ROW), head))

    def spread(values):
        tall = jnp.concatenate([values, jnp.zeros((LANES - 16, run_len), jnp.float32)], axis=0)
        return jnp.transpose(tall).astype(jnp.bfloat16)

    def key_marks(slot):
        km[slot] = spread(info[slot, 0:16].astype(jnp.float32))

    def add_keys(state, q, marks, j, slot):
        top, total, acc = state
        k = kbuf[j, slot].reshape(run_len, HEAD_DIM)
        v = vbuf[j, slot].reshape(run_len, HEAD_DIM)
        if marks is not None:
            q = jnp.concatenate([q, marks], axis=1)
            k = jnp.concatenate([k, km[slot]], axis=1)
        scores = lax.dot_general(k, q, (((1,), (1,)), ((), ())), preferred_element_type=jnp.float32) * factor
        high = jnp.max(scores, axis=0, keepdims=True)
        new = high if top is None else jnp.maximum(top, high)
        weights = jnp.exp2(scores - new)
        part = jnp.sum(weights, axis=0, keepdims=True)
        mixed = lax.dot_general(
            v, weights.astype(jnp.bfloat16), (((0,), (0,)), ((), ())), preferred_element_type=jnp.float32
        )
        if top is None:
            return new, part, mixed
        fade = jnp.exp2(top - new)
        return new, total * fade + part, acc * fade + mixed

    def load(j, run):
        at = lax.rem(j, 2)
        return top_s[at, run][0:1], sum_s[at, run][0:1], acc_s[at, run]

    def store(state, j, run):
        at = lax.rem(j, 2)
        top, total, acc = state
        top_s[at, run] = jnp.broadcast_to(top, (8, half))
        sum_s[at, run] = jnp.broadcast_to(total, (8, half))
        acc_s[at, run] = acc

    def marks_of(side, run, of):
        return qm[side, run, pl.ds(pl.multiple_of(of * half, half), half)]

    def my_queries(j, run):
        return queries_of(j, run)[...].reshape(half, HEAD_DIM)

    def steps(j, slot, pairs):
        states = []
        for run, side in pairs:
            marks = None if side is None else marks_of(side, run, zl)
            states.append(add_keys(load(j, run), my_queries(j, run), marks, j, slot))
        for (run, _), state in zip(pairs, states):
            store(state, j, run)

    def finish(acc, total, j, run):
        rows_first = jnp.transpose(acc / total).astype(jnp.bfloat16)
        obuf[j, pl.ds(2 * run, 2)] = rows_first.reshape(2, rows, HEAD_DIM)
        for c in range(2):
            peer = 2 * run + c

            @pl.when(peer != me)
            def _():
                send(obuf.at[j, peer], out.at[:, columns(me, j)], o_send.at[j], o_recv, device(peer))

            @pl.when(peer == me)
            def _():
                pltpu.make_async_copy(obuf.at[j, peer], out.at[:, columns(me, j)], o_recv).start()

    def finish_run(j, run):
        _, total, acc = load(j, run)
        finish(acc, total, j, run)

    def outer(j):
        @pl.when(j == 0)
        def _():
            wait(info.at[ROW], ih_recv)
            key_marks(ROW)

        for kind, _, buf in sources[:2]:
            wait(buf.at[j, ROW], h_recv.at[kind, j])
        wait(q_far.at[j], q_recv.at[j])
        far = q_far[j].reshape(half, HEAD_DIM)
        top, total, acc = add_keys((None, None, None), far, marks_of(zl, own_edge, 1 - zl), j, ROW)
        state = add_keys(load(j, own_edge), my_queries(j, own_edge), marks_of(zl, own_edge, zl), j, ROW)
        o_far[j] = (acc / total).astype(jnp.bfloat16)
        logs = top + jnp.log2(total)
        packed = jnp.zeros((8, LANES), jnp.float32)
        for g in range(half // LANES):
            packed = jnp.where(log_row == g, logs[:, g * LANES : (g + 1) * LANES], packed)
        log_far[j] = packed
        send(o_far.at[j], o_back.at[j], p_send.at[j], p_recv.at[j], partner)
        send(log_far.at[j], log_back.at[j], l_send.at[j], l_recv.at[j], partner)
        finish(state[2], state[1], j, own_edge)

    def merge(j):
        wait(o_back.at[j], p_recv.at[j])
        wait(log_back.at[j], l_recv.at[j])
        top, total, acc = load(j, far_edge)
        logs = log_back[j]
        log = jnp.concatenate([logs[g : g + 1] for g in range(half // LANES)], axis=1)
        high = jnp.maximum(top, log)
        fade, other = jnp.exp2(top - high), jnp.exp2(log - high)
        finish(acc * fade + o_back[j].astype(jnp.float32) * other, total * fade + other, j, far_edge)

    def mirrored(index, flip):
        return index + flip * (last - 2 * index)

    def send_ahead(j, index):
        z_start(j, mirrored(index, 1 - zl))

        @pl.when(index == 1)
        def _():
            @pl.when(j + 1 < heads)
            def _():
                x_start(j + 1)

        @pl.when(index == last)
        def _():
            q_start(j)

    def ahead_first(index, carry):
        send_ahead(0, index)
        return carry

    lax.fori_loop(0, ROW, ahead_first, 0)

    def drain_early(j, direct):
        for kind, _, buf in sources:
            wait(qbuf.at[j, pl.ds(0, PEERS - 1)], x_send.at[kind, j])
            if kind < 2:
                if direct:
                    wait(qbuf.at[j, pl.ds(0, 2)], d_send.at[kind, j])
                wait(buf.at[j, pl.ds(0, ROW - direct), pl.ds(0, 2)], z_send.at[kind, j])
                wait(buf.at[j, ROW], h_send.at[kind, j])
        wait(q_far.at[j], q_send.at[j])

    def drain_late(j):
        wait(qbuf.at[j, pl.ds(0, PEERS - 1)], o_send.at[j])
        wait(o_far.at[j], p_send.at[j])
        wait(log_far.at[j], l_send.at[j])

    def one_unit(t, carry):
        j = lax.div(t, ROW)
        index = lax.rem(t, ROW)
        run = mirrored(index, zl)

        @pl.when(j + 1 < heads)
        def _():
            send_ahead(j + 1, index)

        @pl.when(t == 0)
        def _():
            wait(info.at[pl.ds(0, ROW - 1)], i_recv)
            send(info.at[own_edge], info.at[ROW], ih_send, ih_recv, mate)
            for r in range(ROW):
                key_marks(r)
                marks = info[r, 16:32].astype(jnp.float32)
                qm[0, r] = spread(jnp.where(which < 2, marks, 0.0))
                qm[1, r] = spread(jnp.where(which >= 2, marks, 0.0))

        @pl.when(index == 0)
        def _():
            at = lax.rem(j, 2)
            top_s[at] = jnp.full((ROW, 8, half), 4.0 * HIDE, jnp.float32)
            sum_s[at] = jnp.zeros((ROW, 8, half), jnp.float32)
            acc_s[at] = jnp.zeros((ROW, HEAD_DIM, half), jnp.float32)

        @pl.when((index == 1) & (j > 0))
        def _():
            drain_early(j - 1, 1)

        @pl.when((index == 1) & (j > 1))
        def _():
            drain_late(j - 2)

        @pl.when((index == 2) & (j > 0))
        def _():
            merge(j - 1)

        @pl.when(index == 2)
        def _():
            outer(j)

        for kind, _, buf in sources[:2]:
            wait(unit(buf, j, run, 1 - zl), z_recv.at[kind, j, run])

        @pl.when(index == 0)
        def _():
            for kind, _, buf in sources[:2]:
                halo_start(kind, buf, j, 1 - zl)

        ahead, behind = (run + 1 - 2 * zl, zl), (run - 1 + 2 * zl, 1 - zl)

        @pl.when(index == 0)
        def _():
            steps(j, run, [ahead, (run, None)])

        @pl.when((index > 0) & (index < last))
        def _():
            steps(j, run, [behind, ahead, (run, None)])

        @pl.when(index == last)
        def _():
            steps(j, run, [behind, (run, None)])

        @pl.when(index >= 2)
        def _():
            finish_run(j, mirrored(index - 1, zl))

        return carry

    lax.fori_loop(0, heads * ROW, one_unit, 0)
    drain_early(heads - 1, 0)
    if heads > 1:
        drain_late(heads - 2)
    wait(info.at[pl.ds(0, ROW - 1)], i_send)
    wait(info.at[0], ih_send)
    merge(heads - 1)
    drain_late(heads - 1)
    wait(out, o_recv)


def local(queries, key_input, value_input, token_order, tile_mask):
    rows, width = queries.shape
    heads = width // HEAD_DIM // PEERS
    runs = lax.axis_size("blk")
    run_len = 4 * rows
    half = 2 * rows
    bf16, f32 = jnp.bfloat16, jnp.float32
    dma = pltpu.SemaphoreType.DMA
    hbm = pl.BlockSpec(memory_space=pl.ANY)
    vmem = pl.BlockSpec(memory_space=pltpu.VMEM)
    flops = 4 * heads * ROW * half * 3 * run_len * HEAD_DIM
    return pl.pallas_call(
        functools.partial(kernel, heads, runs),
        out_shape=jax.ShapeDtypeStruct(queries.shape, queries.dtype),
        in_specs=[hbm, hbm, hbm, vmem, vmem],
        out_specs=hbm,
        scratch_shapes=[
            pltpu.VMEM((heads, ROW + 1, 4, rows, HEAD_DIM), bf16),
            pltpu.VMEM((heads, ROW + 1, 4, rows, HEAD_DIM), bf16),
            pltpu.VMEM((heads, PEERS, rows, HEAD_DIM), bf16),
            pltpu.VMEM((heads, PEERS, rows, HEAD_DIM), bf16),
            pltpu.VMEM((heads, 2, rows, HEAD_DIM), bf16),
            pltpu.VMEM((heads, HEAD_DIM, half), bf16),
            pltpu.VMEM((heads, HEAD_DIM, half), bf16),
            pltpu.VMEM((heads, 8, LANES), f32),
            pltpu.VMEM((heads, 8, LANES), f32),
            pltpu.VMEM((ROW + 1, 32, run_len), bf16),
            pltpu.VMEM((ROW + 1, run_len, LANES), bf16),
            pltpu.VMEM((2, ROW, run_len, LANES), bf16),
            pltpu.VMEM((2, ROW, 8, half), f32),
            pltpu.VMEM((2, ROW, 8, half), f32),
            pltpu.VMEM((2, ROW, HEAD_DIM, half), f32),
            dma((3, heads, ROW)), dma((3, heads)),
            dma((2, heads, ROW)), dma((2, heads)), dma((2, heads)),
            dma((2, heads)), dma((2, heads)),
            dma, dma((heads,)),
            dma, dma, dma, dma,
            dma((heads,)), dma((heads,)),
            dma((heads,)), dma((heads,)),
            dma((heads,)), dma((heads,)),
        ],
        compiler_params=pltpu.CompilerParams(
            collective_id=0, has_side_effects=True, vmem_limit_bytes=56 * 1024 * 1024
        ),
        cost_estimate=pl.CostEstimate(
            flops=flops, bytes_accessed=8 * rows * width, transcendentals=flops // (4 * HEAD_DIM)
        ),
    )(queries, key_input, value_input, token_order, tile_mask)


def solution(mesh):
    in_specs = (
        P(("blk", "head"), None),
        P(("blk", "head"), None),
        P(("blk", "head"), None),
        P("blk"),
        P("blk", None),
    )
    out_specs = P(("blk", "head"), None)
    return jax.shard_map(local, mesh=mesh, in_specs=in_specs, out_specs=out_specs, check_vma=False)
```

time: 137 us -> 131 us (0.956)
  Pallas kernels: 132 us -> 128 us
    pallas_call x1, Pallas kernels: 132 us -> 128 us  [local(): pl.pallas_call(functools.partial(kernel, heads, runs), out_shape=jax.Shap...]
where the time goes in v3:
time: 131 us
  Pallas kernels  128 us (98%)
  local copies, waits for them, and re-layouts  2.94 us (2%)
    pallas_call x1, Pallas kernels, local(): pl.pallas_call(functools.partial(kernel, heads, runs), out_shape=jax.Shap...  128 us
    unnamed x1, local copies, waits for them, and re-layouts  2.94 us

profile of v3, /device:TPU:33, one launch (start us, length us, event | category | flops | bytes accessed | tf_op | source)
XLA Modules:
  0.0 131.0 jit_solution(15061822130180862230)
XLA Ops:
  0.0 128.1 %shard_map.55 = bf16[192,5120]{1,0:T(8,128)(2,1)} custom-call(bf16[192,5120]{1,0:T(8,128)(2,1)} %q_in.1, bf16[192,5120]{1,0:T(8,128)(2,1)} %k_in.1, bf16[192,5120]{1,0:T(8,128)(2,1)} %v_in.1, s32[768]{0:T(1024)} %order_ref.1, s32[2,128]{1,0:T(2,128)} %mask_ref.1), custom_call_target="tpu_custom_call" | custom-call | flops 9059696640 | bytes 7864320 | tf_op jit(solution)/shard_map/pallas_call | solution.py:389
  128.1 2.9 %copy.7 = bf16[192,5120]{1,0:T(8,128)(2,1)} copy(bf16[192,5120]{1,0:T(8,128)(2,1)} %shard_map.55) | data formatting | bytes 3932160

commit v4 on v3

--- a/solution.py
+++ b/solution.py
@@ -18,11 +18,11 @@
 
 def kernel(
     heads, runs,
-    q_in, k_in, v_in, order_ref, mask_ref,
+    q_in, k_in, v_in, order_in, mask_in,
     out,
     kbuf, vbuf, qbuf, obuf, q_far, o_far, o_back, log_far, log_back, info, km, qm, top_s, sum_s, acc_s,
     x_recv, x_send, z_recv, z_send, d_send, h_recv, h_send, o_recv, o_send, i_recv, i_send, ih_recv, ih_send,
-    q_recv, q_send, p_recv, p_send, l_recv, l_send,
+    q_recv, q_send, p_recv, p_send, l_recv, l_send, order_ref, mask_ref, tile_sem,
 ):
     rows = q_in.shape[0]
     run_len = 4 * rows
@@ -55,6 +55,13 @@
     for to in greet:
         pl.semaphore_signal(barrier, inc=1, device_id=to, device_id_type=MESH)
 
+    order_copy = pltpu.make_async_copy(order_in, order_ref, tile_sem.at[0])
+    mask_copy = pltpu.make_async_copy(mask_in, mask_ref, tile_sem.at[1])
+    order_copy.start()
+    mask_copy.start()
+    order_copy.wait()
+    mask_copy.wait()
+
     order = (order_ref[...].reshape(1, run_len) - blk * run_len).astype(jnp.float32)
     order = jnp.transpose(jnp.broadcast_to(order, (LANES, run_len)))[half:]
     lane = lax.broadcasted_iota(jnp.int32, (half, LANES), 1).astype(jnp.float32)
@@ -126,7 +133,9 @@
 
     def z_start(j, run):
         for kind, _, buf in sources[:2]:
-            wait(unit(buf, j, run, zl), x_recv.at[kind, j, run])
+            @pl.when(run != own_edge)
+            def _():
+                wait(unit(buf, j, run, zl), x_recv.at[kind, j, run])
 
             @pl.when((run != x) | (j == heads - 1))
             def _():
@@ -134,10 +143,6 @@
                     unit(buf, j, run, zl), unit(buf, j, run, zl),
                     z_send.at[kind, j], z_recv.at[kind, j, run], partner,
                 )
-
-            @pl.when(run == own_edge)
-            def _():
-                halo_start(kind, buf, j, zl)
 
     def queries_of(j, run):
         return qbuf.at[j, pl.ds(2 * run, 2)]
@@ -261,17 +266,21 @@
         return index + flip * (last - 2 * index)
 
     def send_ahead(j, index):
+        @pl.when(index == 0)
+        def _():
+            for kind, _, buf in sources[:2]:
+                wait(unit(buf, j, own_edge, zl), x_recv.at[kind, j, own_edge])
+                halo_start(kind, buf, j, zl)
+
         z_start(j, mirrored(index, 1 - zl))
 
-        @pl.when(index == 1)
-        def _():
+        @pl.when(index == 0)
+        def _():
+            q_start(j)
+
             @pl.when(j + 1 < heads)
             def _():
                 x_start(j + 1)
-
-        @pl.when(index == last)
-        def _():
-            q_start(j)
 
     def ahead_first(index, carry):
         send_ahead(0, index)
@@ -388,9 +397,9 @@
     flops = 4 * heads * ROW * half * 3 * run_len * HEAD_DIM
     return pl.pallas_call(
         functools.partial(kernel, heads, runs),
-        out_shape=jax.ShapeDtypeStruct(queries.shape, queries.dtype),
-        in_specs=[hbm, hbm, hbm, vmem, vmem],
-        out_specs=hbm,
+        out_shape=pltpu.VMEM(queries.shape, queries.dtype),
+        in_specs=[hbm] * 5,
+        out_specs=vmem,
         scratch_shapes=[
             pltpu.VMEM((heads, ROW + 1, 4, rows, HEAD_DIM), bf16),
             pltpu.VMEM((heads, ROW + 1, 4, rows, HEAD_DIM), bf16),
@@ -415,6 +424,9 @@
             dma((heads,)), dma((heads,)),
             dma((heads,)), dma((heads,)),
             dma((heads,)), dma((heads,)),
+            pltpu.VMEM(token_order.shape, token_order.dtype),
+            pltpu.VMEM(tile_mask.shape, tile_mask.dtype),
+            dma((2,)),
         ],
         compiler_params=pltpu.CompilerParams(
             collective_id=0, has_side_effects=True, vmem_limit_bytes=56 * 1024 * 1024

time: 131 us -> 125 us (0.954)
  Pallas kernels: 128 us -> 124 us
  local copies, waits for them, and re-layouts: 2.94 us -> 1.27 us
    pallas_call x1, Pallas kernels: 128 us -> 124 us  [local(): pl.pallas_call(functools.partial(kernel, heads, runs), out_shape=pltpu.VM...]
    unnamed x1, local copies, waits for them, and re-layouts: 2.94 us -> 1.27 us
where the time goes in v4:
time: 125 us
  Pallas kernels  124 us (99%)
  local copies, waits for them, and re-layouts  1.27 us (1%)
    pallas_call x1, Pallas kernels, local(): pl.pallas_call(functools.partial(kernel, heads, runs), out_shape=pltpu.VM...  124 us

profile of v4, /device:TPU:33, one launch (start us, length us, event | category | flops | bytes accessed | tf_op | source)
XLA Modules:
  0.0 125.0 jit_solution(17750825861069467113)
XLA Ops:
  0.0 123.7 %shard_map.55 = bf16[192,5120]{1,0:T(8,128)(2,1)S(1)} custom-call(bf16[192,5120]{1,0:T(8,128)(2,1)} %q_in.1, bf16[192,5120]{1,0:T(8,128)(2,1)} %k_in.1, bf16[192,5120]{1,0:T(8,128)(2,1)} %v_in.1, s32[768]{0:T(1024)} %order_in.1, s32[2,128]{1,0:T(2,128)} %mask_in.1), custom_call_target="tpu_custom_call" | custom-call | flops 9059696640 | bytes 7864320 | tf_op jit(solution)/shard_map/pallas_call | solution.py:398
  123.7 1.3 %copy.7 = bf16[192,5120]{1,0:T(8,128)(2,1)} copy(bf16[192,5120]{1,0:T(8,128)(2,1)S(1)} %shard_map.55) | data formatting | bytes 3932160

commit v5 on v4

--- a/solution.py
+++ b/solution.py
@@ -274,7 +274,7 @@
 
         z_start(j, mirrored(index, 1 - zl))
 
-        @pl.when(index == 0)
+        @pl.when(index == 1)
         def _():
             q_start(j)
 
@@ -374,12 +374,12 @@
         return carry
 
     lax.fori_loop(0, heads * ROW, one_unit, 0)
+    merge(heads - 1)
     drain_early(heads - 1, 0)
     if heads > 1:
         drain_late(heads - 2)
     wait(info.at[pl.ds(0, ROW - 1)], i_send)
     wait(info.at[0], ih_send)
-    merge(heads - 1)
     drain_late(heads - 1)
     wait(out, o_recv)
 

time: 125 us -> 125 us (level)
  no operation moved by 1% of the time
where the time goes in v5:
time: 125 us
  Pallas kernels  123 us (98%)
  local copies, waits for them, and re-layouts  1.27 us (1%)
    pallas_call x1, Pallas kernels, local(): pl.pallas_call(functools.partial(kernel, heads, runs), out_shape=pltpu.VM...  123 us

profile of v5, /device:TPU:33, one launch (start us, length us, event | category | flops | bytes accessed | tf_op | source)
XLA Modules:
  0.0 124.8 jit_solution(16453333493094063811)
XLA Ops:
  0.0 123.5 %shard_map.55 = bf16[192,5120]{1,0:T(8,128)(2,1)S(1)} custom-call(bf16[192,5120]{1,0:T(8,128)(2,1)} %q_in.1, bf16[192,5120]{1,0:T(8,128)(2,1)} %k_in.1, bf16[192,5120]{1,0:T(8,128)(2,1)} %v_in.1, s32[768]{0:T(1024)} %order_in.1, s32[2,128]{1,0:T(2,128)} %mask_in.1), custom_call_target="tpu_custom_call" | custom-call | flops 9059696640 | bytes 7864320 | tf_op jit(solution)/shard_map/pallas_call | solution.py:398
  123.5 1.3 %copy.7 = bf16[192,5120]{1,0:T(8,128)(2,1)} copy(bf16[192,5120]{1,0:T(8,128)(2,1)S(1)} %shard_map.55) | data formatting | bytes 3932160

commit v6 on v5

--- a/solution.py
+++ b/solution.py
@@ -59,6 +59,72 @@
     mask_copy = pltpu.make_async_copy(mask_in, mask_ref, tile_sem.at[1])
     order_copy.start()
     mask_copy.start()
+    pl.semaphore_wait(barrier, len(greet))
+
+    def columns(peer, j):
+        return pl.ds(pl.multiple_of((heads * peer + j) * HEAD_DIM, HEAD_DIM), HEAD_DIM)
+
+    def send(src, dst, send_sem, recv_sem, to):
+        pltpu.make_async_remote_copy(
+            src_ref=src, dst_ref=dst, send_sem=send_sem, recv_sem=recv_sem, device_id=to, device_id_type=MESH
+        ).start()
+
+    def wait(like, sem):
+        pltpu.make_async_copy(like, like, sem).wait()
+
+    sources = ((0, k_in, kbuf), (1, v_in, vbuf), (2, q_in, qbuf))
+
+    def direct_start(j):
+        for kind, source, buf in sources[:2]:
+            for c in range(2):
+                send(
+                    source.at[:, columns(2 * x + c, j)], buf.at[j, x, head],
+                    d_send.at[kind, j], z_recv.at[kind, j, x], (blk, across + c),
+                )
+
+    def x_start(j):
+        for kind, source, buf in sources:
+            place = qbuf.at[j, me] if kind == 2 else buf.at[j, x, head]
+            pltpu.make_async_copy(source.at[:, columns(me, j)], place, x_recv.at[kind, j, x]).start()
+            for step in range(1, PEERS):
+                peer = peer_at(step)
+                send(
+                    source.at[:, columns(peer, j)], place,
+                    x_send.at[kind, j], x_recv.at[kind, j, x], device(peer),
+                )
+
+    def unit(buf, j, run, side):
+        return buf.at[j, run, pl.ds(2 * side, 2)]
+
+    def halo_start(kind, buf, j, side):
+        send(unit(buf, j, own_edge, side), unit(buf, j, ROW, side), h_send.at[kind, j], h_recv.at[kind, j], mate)
+
+    def z_start(j, run):
+        for kind, _, buf in sources[:2]:
+            @pl.when(run != own_edge)
+            def _():
+                wait(unit(buf, j, run, zl), x_recv.at[kind, j, run])
+
+            @pl.when((run != x) | (j == heads - 1))
+            def _():
+                send(
+                    unit(buf, j, run, zl), unit(buf, j, run, zl),
+                    z_send.at[kind, j], z_recv.at[kind, j, run], partner,
+                )
+
+    def queries_of(j, run):
+        return qbuf.at[j, pl.ds(2 * run, 2)]
+
+    def q_start(j):
+        for run in range(ROW):
+            wait(queries_of(j, run), x_recv.at[2, j, run])
+        send(queries_of(j, far_edge), q_far.at[j], q_send.at[j], q_recv.at[j], partner)
+
+    direct_start(0)
+    x_start(0)
+    for j in range(1, heads - 1):
+        direct_start(j)
+
     order_copy.wait()
     mask_copy.wait()
 
@@ -91,71 +157,6 @@
     mine = info.at[x]
     mine[0:16] = stack((1.0 - second, second, 1.0 - second, second))
     mine[16:32] = stack((bias(-2), bias(-1), bias(2), bias(3)))
-    pl.semaphore_wait(barrier, len(greet))
-
-    def columns(peer, j):
-        return pl.ds(pl.multiple_of((heads * peer + j) * HEAD_DIM, HEAD_DIM), HEAD_DIM)
-
-    def send(src, dst, send_sem, recv_sem, to):
-        pltpu.make_async_remote_copy(
-            src_ref=src, dst_ref=dst, send_sem=send_sem, recv_sem=recv_sem, device_id=to, device_id_type=MESH
-        ).start()
-
-    def wait(like, sem):
-        pltpu.make_async_copy(like, like, sem).wait()
-
-    sources = ((0, k_in, kbuf), (1, v_in, vbuf), (2, q_in, qbuf))
-
-    def direct_start(j):
-        for kind, source, buf in sources[:2]:
-            for c in range(2):
-                send(
-                    source.at[:, columns(2 * x + c, j)], buf.at[j, x, head],
-                    d_send.at[kind, j], z_recv.at[kind, j, x], (blk, across + c),
-                )
-
-    def x_start(j):
-        for kind, source, buf in sources:
-            place = qbuf.at[j, me] if kind == 2 else buf.at[j, x, head]
-            pltpu.make_async_copy(source.at[:, columns(me, j)], place, x_recv.at[kind, j, x]).start()
-            for step in range(1, PEERS):
-                peer = peer_at(step)
-                send(
-                    source.at[:, columns(peer, j)], place,
-                    x_send.at[kind, j], x_recv.at[kind, j, x], device(peer),
-                )
-
-    def unit(buf, j, run, side):
-        return buf.at[j, run, pl.ds(2 * side, 2)]
-
-    def halo_start(kind, buf, j, side):
-        send(unit(buf, j, own_edge, side), unit(buf, j, ROW, side), h_send.at[kind, j], h_recv.at[kind, j], mate)
-
-    def z_start(j, run):
-        for kind, _, buf in sources[:2]:
-            @pl.when(run != own_edge)
-            def _():
-                wait(unit(buf, j, run, zl), x_recv.at[kind, j, run])
-
-            @pl.when((run != x) | (j == heads - 1))
-            def _():
-                send(
-                    unit(buf, j, run, zl), unit(buf, j, run, zl),
-                    z_send.at[kind, j], z_recv.at[kind, j, run], partner,
-                )
-
-    def queries_of(j, run):
-        return qbuf.at[j, pl.ds(2 * run, 2)]
-
-    def q_start(j):
-        for run in range(ROW):
-            wait(queries_of(j, run), x_recv.at[2, j, run])
-        send(queries_of(j, far_edge), q_far.at[j], q_send.at[j], q_recv.at[j], partner)
-
-    direct_start(0)
-    x_start(0)
-    for j in range(1, heads - 1):
-        direct_start(j)
 
     for step in range(1, ROW):
         send(mine, mine, i_send, i_recv, (first + lax.rem(x + step, ROW), head))
@@ -241,7 +242,6 @@
         wait(q_far.at[j], q_recv.at[j])
         far = q_far[j].reshape(half, HEAD_DIM)
         top, total, acc = add_keys((None, None, None), far, marks_of(zl, own_edge, 1 - zl), j, ROW)
-        state = add_keys(load(j, own_edge), my_queries(j, own_edge), marks_of(zl, own_edge, zl), j, ROW)
         o_far[j] = (acc / total).astype(jnp.bfloat16)
         logs = top + jnp.log2(total)
         packed = jnp.zeros((8, LANES), jnp.float32)
@@ -250,6 +250,7 @@
         log_far[j] = packed
         send(o_far.at[j], o_back.at[j], p_send.at[j], p_recv.at[j], partner)
         send(log_far.at[j], log_back.at[j], l_send.at[j], l_recv.at[j], partner)
+        state = add_keys(load(j, own_edge), my_queries(j, own_edge), marks_of(zl, own_edge, zl), j, ROW)
         finish(state[2], state[1], j, own_edge)
 
     def merge(j):

time: 125 us -> 125 us (level)
  no operation moved by 1% of the time
where the time goes in v6:
time: 125 us
  Pallas kernels  123 us (98%)
  local copies, waits for them, and re-layouts  1.27 us (1%)
    pallas_call x1, Pallas kernels, local(): pl.pallas_call(functools.partial(kernel, heads, runs), out_shape=pltpu.VM...  123 us

profile of v6, /device:TPU:33, one launch (start us, length us, event | category | flops | bytes accessed | tf_op | source)
XLA Modules:
  0.0 124.8 jit_solution(12198875881671445104)
XLA Ops:
  0.0 123.5 %shard_map.55 = bf16[192,5120]{1,0:T(8,128)(2,1)S(1)} custom-call(bf16[192,5120]{1,0:T(8,128)(2,1)} %q_in.1, bf16[192,5120]{1,0:T(8,128)(2,1)} %k_in.1, bf16[192,5120]{1,0:T(8,128)(2,1)} %v_in.1, s32[768]{0:T(1024)} %order_in.1, s32[2,128]{1,0:T(2,128)} %mask_in.1), custom_call_target="tpu_custom_call" | custom-call | flops 9059696640 | bytes 7864320 | tf_op jit(solution)/shard_map/pallas_call | solution.py:399
  123.5 1.3 %copy.7 = bf16[192,5120]{1,0:T(8,128)(2,1)} copy(bf16[192,5120]{1,0:T(8,128)(2,1)S(1)} %shard_map.55) | data formatting | bytes 3932160
